TPU v7x, 32 devices: a whole 2x2x4 slice. The times are simulated.
32 devices in a mesh: sec: 2 (over x), cpl: 2 (over y), dom: 8 (over z, core).
Axes of the slice: x: 2, y: 2, z: 4, core: 2. Of those that a mesh axis runs over, the one named last changes fastest.
Arguments:
- component_fields: float32 [2, 24, 65536], P('sec', None, 'dom'), may hold values from -6 to 6
- wet_mask: int32 [2, 65536], P('sec', 'dom'), may hold values 0 or 1
- state_tiles: bfloat16 [2, 384, 128, 128], P('sec', ('cpl', 'dom')), may hold values from -0.625 to 0.625
- state_source: int32 [2, 384], P('sec', ('cpl', 'dom')), may hold values from 0 to 79
- state_target: int32 [2, 384], P('sec', ('cpl', 'dom')), may hold values from 0 to 63
- flux_tiles: bfloat16 [2, 384, 128, 128], P('sec', ('cpl', 'dom')), may hold values from -0.625 to 0.625
- flux_source: int32 [2, 384], P('sec', ('cpl', 'dom')), may hold values from 0 to 79
- flux_target: int32 [2, 384], P('sec', ('cpl', 'dom')), may hold values from 0 to 63
Outputs:
- delivered: float32 [2, 24, 65536], P('sec', None, 'dom')
- fluxes: float32 [2, 8, 65536], P('sec', None, 'dom')
Inputs may be any that keep to these rules, and one draw needn't show every extreme that they name: `state_source`: a tile's source block counts the last 8 blocks of the dom index before the tile's own, then its own 64, then the first 8 of the one after, wrapping around. `flux_source`: as for state_source. `state_target`: a destination block among the 64 blocks of the other grid that share the tile's dom index. `flux_target`: as for state_target.
All inputs are finite; a program needn't handle non-finite values. No bound on the sum of `wet_mask` on one device may be relied on, other than what follows from the above.
Results may differ from a plain program's by a relative error of at most 0.0037.
Values may be sent and summed in bfloat16 or wider, within the bound.
A program may use at most 64 MiB of HBM per device.

v0:
```python
import jax
import jax.numpy as jnp
from jax import lax
from jax.sharding import PartitionSpec as P

TILE = 128
BULK_ITERS = 3
RIM = 8


def extended_2(block, sides, width):
    for axis, dim in sides:
        count = lax.axis_size(axis)
        forward = [(i, i + 1) for i in range(count - 1)]
        forward.append((count - 1, 0))
        backward = [(target, source) for source, target in forward]
        low = lax.ppermute(
            lax.slice_in_dim(block, block.shape[dim] - width, None, axis=dim), axis, forward
        )
        high = lax.ppermute(lax.slice_in_dim(block, 0, width, axis=dim), axis, backward)
        block = jnp.concatenate([low, block, high], axis=dim)
    return block


def swapped(block, axis, bit):
    count = lax.axis_size(axis)
    route = []
    for low in range(count):
        high = low | 1 << bit
        if high != low and high < count:
            route += [(low, high), (high, low)]
    return lax.ppermute(block, axis, route)


def remap_local(extended, weights, source, target, local_blocks):
    row_count = extended.shape[0]
    blocks = extended.reshape(row_count, local_blocks + 2 * RIM, TILE)
    pieces = jnp.take(blocks, source, axis=1)
    product = jnp.einsum("rti,tij->rtj", pieces, weights, preferred_element_type=jnp.float32)
    placed = jnp.zeros((row_count, local_blocks, TILE), jnp.float32).at[:, target].add(product)
    return placed.reshape(row_count, local_blocks * TILE)


def bulk_flux(atmos, ocean, wet_frac):
    wind_u = atmos[0] - ocean[0]
    wind_v = atmos[1] - ocean[1]
    wind_speed = jnp.sqrt(wind_u * wind_u + wind_v * wind_v + 0.5)
    temp_diff = atmos[2] - ocean[2]
    humid_diff = atmos[3] - 0.5 * ocean[3]
    neutral = 1.0 + 0.5 * jnp.tanh(atmos[4] + ocean[4])
    richardson = 2.0 * temp_diff / (wind_speed * wind_speed)
    drag_coef = neutral
    for _ in range(BULK_ITERS):
        drag_coef = neutral * (1.0 + 0.8 * jnp.tanh(-richardson * drag_coef))
    transfer = drag_coef * wind_speed
    stacked = jnp.stack(
        [
            0.5 * transfer * wind_u,
            0.5 * transfer * wind_v,
            0.5 * transfer * temp_diff,
            0.5 * transfer * humid_diff,
            atmos[5] * (1.0 - 0.3 * jnp.tanh(ocean[5])),
            atmos[6] - 0.5 * ocean[2],
            atmos[7] - 0.15 * transfer * humid_diff,
            0.5 * jnp.sqrt(drag_coef) * wind_speed,
        ]
    )
    return stacked * wet_frac[None, :]


def body(
    component_fields,
    wet_mask,
    state_tiles,
    state_source,
    state_target,
    flux_tiles,
    flux_source,
    flux_target,
):
    own_fields = component_fields[0]
    wet_frac = wet_mask[0].astype(jnp.float32)
    cell_count = own_fields.shape[1]
    local_blocks = cell_count // TILE
    extended = extended_2(own_fields.astype(jnp.bfloat16), (("dom", 1),), RIM * TILE)
    partial_sum = remap_local(
        extended, state_tiles[0], state_source[0], state_target[0], local_blocks
    )
    share_part = lax.psum_scatter(partial_sum, "cpl", scatter_dimension=1, tiled=True)
    crossed = swapped(share_part, "sec", 0)
    received = lax.all_gather(crossed, "cpl", axis=1, tiled=True)
    first_sec = lax.axis_index("sec") == 0
    atmos = jnp.where(first_sec, own_fields, received)
    ocean = jnp.where(first_sec, received, own_fields)
    flux_own = bulk_flux(atmos, ocean, wet_frac)
    flux_ext = extended_2(flux_own.astype(jnp.bfloat16), (("dom", 1),), RIM * TILE)
    flux_part = remap_local(flux_ext, flux_tiles[0], flux_source[0], flux_target[0], local_blocks)
    flux_share = lax.psum_scatter(flux_part, "cpl", scatter_dimension=1, tiled=True)
    flux_crossed = swapped(flux_share, "sec", 0)
    flux_back = lax.all_gather(flux_crossed, "cpl", axis=1, tiled=True)
    merged = 0.5 * (flux_own + wet_frac[None, :] * flux_back)
    return (received[None], merged[None])


def solution(mesh):
    return jax.shard_map(
        body,
        mesh=mesh,
        in_specs=(
            P("sec", None, "dom"),
            P("sec", "dom"),
            P("sec", ("cpl", "dom"), None, None),
            P("sec", ("cpl", "dom")),
            P("sec", ("cpl", "dom")),
            P("sec", ("cpl", "dom"), None, None),
            P("sec", ("cpl", "dom")),
            P("sec", ("cpl", "dom")),
        ),
        out_specs=(P("sec", None, "dom"), P("sec", None, "dom")),
        check_vma=False,
    )
```

profile of v0, /device:TPU:0, one launch (start us, length us, event | category | flops | bytes accessed | tf_op | source)
XLA Modules:
  0.0 101.5 jit_solution(12307826315681400025)
XLA Ops:
  7.2 1.2 %bitcast_convert_fusion = bf16[24,8192]{1,0:T(8,128)(2,1)S(1)} fusion(f32[1,24,8192]{2,1,0:T(8,128)} %param.8), kind=kLoop, calls=%fused_computation.11 | loop fusion | flops 196608 | bytes 1179648 | tf_op jit(solution)/shard_map/convert_element_type | solution.py:85
  8.5 0.5 collective-permute-start
  9.0 4.1 %collective-permute-start.1 = (bf16[24,1024]{1,0:T(8,128)(2,1)S(1)}, bf16[24,1024]{1,0:T(8,128)(2,1)S(1)}, u32[]{:S(2)}, u32[]{:S(2)}) collective-permute-start(bf16[24,1024]{1,0:T(8,128)(2,1)S(1)} %get-tuple-element.19), channel_id=1, source_target_pairs={{1,0},{2,1},{3,2},{4,3},{5,4},{6,5},{7,6},{0,7},{9,8},{10,9},{11,1... | collective-permute-start | bytes 147464 | tf_op jit(solution)/shard_map/ppermute | solution.py:20
  13.1 0.6 copy-done.6
  13.8 1.0 %collective-permute-done = bf16[24,1024]{1,0:T(8,128)(2,1)S(1)} collective-permute-done((bf16[24,1024]{1,0:T(8,128)(2,1)S(1)}, bf16[24,1024]{1,0:T(8,128)(2,1)S(1)}, u32[]{:S(2)}, u32[]{:S(2)}) %collective-permute-start) | collective-permute-done | bytes 49184 | tf_op jit(solution)/shard_map/ppermute | solution.py:17
  14.9 0.1 copy_bitcast_fusion.1
  14.9 0.6 gather_fusion
  15.5 0.4 fusion.2
  16.0 1.9 %scatter_fusion = f32[24,64,128]{2,0,1:T(8,128)S(1)} fusion(f32[24,64,128]{2,0,1:T(8,128)S(1)} %broadcast_in_dim.36, s32[24]{0:T(128)S(1)} %fusion.17, f32[24,24,128]{2,1,0:T(8,128)S(1)} %fusion.2), kind=kCustom, calls=%fused_computation.2 | custom fusion | flops 73728 | bytes 884832 | tf_op jit(solution)/shard_map/scatter-add | solution.py:40
  17.9 0.9 copy_bitcast_fusion
  19.0 0.7 copy-done.4
  19.7 18.5 %reduce-scatter.3.cloned.1.call-done = f32[24,4096]{1,0:T(8,128)} async-done(((f32[24,8192]{1,0:T(8,128)}), f32[24,4096]{1,0:T(8,128)}) %reduce-scatter.3.cloned.1.call-update) | async-done | bytes 393232 | tf_op jit(solution)/shard_map/reduce_scatter | solution.py:89
  38.2 1.5 %collective-permute-start.2 = (f32[24,4096]{1,0:T(8,128)}, f32[24,4096]{1,0:T(8,128)S(1)}, u32[]{:S(2)}, u32[]{:S(2)}) collective-permute-start(f32[24,4096]{1,0:T(8,128)} %reduce-scatter.3.cloned.1.call-done), channel_id=1, source_target_pairs={{0,16},{16,0},{1,17},{17,1},{2,18},{18,2},{3,19},{19,3},{4,20},{20... | collective-permute-start | bytes 1179656 | tf_op jit(solution)/shard_map/ppermute | solution.py:32
  39.7 9.6 %collective-permute-done.2 = f32[24,4096]{1,0:T(8,128)S(1)} collective-permute-done((f32[24,4096]{1,0:T(8,128)}, f32[24,4096]{1,0:T(8,128)S(1)}, u32[]{:S(2)}, u32[]{:S(2)}) %collective-permute-start.2) | collective-permute-done | bytes 393248 | tf_op jit(solution)/shard_map/ppermute | solution.py:32
  49.2 10.6 %all_gather.6 = f32[24,8192]{1,0:T(8,128)S(1)} all-gather(f32[24,4096]{1,0:T(8,128)S(1)} %collective-permute-done.2), channel_id=1, replica_groups=mesh['sec'=2,'cpl'=2,'dom'=8] {'cpl'}, dimensions={1}, use_global_device_ids=true | all-gather | bytes 1179648 | tf_op jit(solution)/shard_map/all_gather | solution.py:91
  59.8 0.2 bitcast_select_fusion.1
  60.0 0.5 multiply_multiply_fusion
  60.6 0.3 slice_subtract_fusion.1
  60.8 0.1 fusion.23
  61.0 0.4 stack.2
  61.5 3.5 %collective-permute-start.4 = (bf16[8,1024]{1,0:T(8,128)(2,1)S(1)}, bf16[8,1024]{1,0:T(8,128)(2,1)S(1)}, u32[]{:S(2)}, u32[]{:S(2)}) collective-permute-start(bf16[8,1024]{1,0:T(8,128)(2,1)S(1)} %get-tuple-element.21), channel_id=1, source_target_pairs={{1,0},{2,1},{3,2},{4,3},{5,4},{6,5},{7,6},{0,7},{9,8},{10,9},{11,1... | collective-permute-start | bytes 49160 | tf_op jit(solution)/shard_map/ppermute | solution.py:20
  65.0 1.4 %collective-permute-done.3 = bf16[8,1024]{1,0:T(8,128)(2,1)S(1)} collective-permute-done((bf16[8,1024]{1,0:T(8,128)(2,1)S(1)}, bf16[8,1024]{1,0:T(8,128)(2,1)S(1)}, u32[]{:S(2)}, u32[]{:S(2)}) %collective-permute-start.3) | collective-permute-done | bytes 16416 | tf_op jit(solution)/shard_map/ppermute | solution.py:17
  66.5 0.6 gather_fusion.1
  67.1 0.4 fusion
  67.5 1.7 %scatter_fusion.1 = f32[8,64,128]{2,0,1:T(8,128)S(1)} fusion(f32[8,64,128]{2,0,1:T(8,128)S(1)} %broadcast_in_dim.40, s32[24]{0:T(128)S(1)} %fusion.19, f32[24,8,128]{2,1,0:T(8,128)S(1)} %fusion), kind=kCustom, calls=%fused_computation.3 | custom fusion | flops 24576 | bytes 295008 | tf_op jit(solution)/shard_map/scatter-add | solution.py:40
  69.2 0.7 copy-done.2
  69.9 12.1 %reduce-scatter.5.cloned.1.call-done = f32[8,4096]{1,0:T(8,128)} async-done(((f32[8,8192]{1,0:T(8,128)}), f32[8,4096]{1,0:T(8,128)}) %reduce-scatter.5.cloned.1.call-update) | async-done | bytes 131088 | tf_op jit(solution)/shard_map/reduce_scatter | solution.py:98
  82.0 1.5 %collective-permute-start.5 = (f32[8,4096]{1,0:T(8,128)}, f32[8,4096]{1,0:T(8,128)S(1)}, u32[]{:S(2)}, u32[]{:S(2)}) collective-permute-start(f32[8,4096]{1,0:T(8,128)} %reduce-scatter.5.cloned.1.call-done), channel_id=1, source_target_pairs={{0,16},{16,0},{1,17},{17,1},{2,18},{18,2},{3,19},{19,3},{4,20},{20... | collective-permute-start | bytes 393224 | tf_op jit(solution)/shard_map/ppermute | solution.py:32
  83.5 4.0 %collective-permute-done.5 = f32[8,4096]{1,0:T(8,128)S(1)} collective-permute-done((f32[8,4096]{1,0:T(8,128)}, f32[8,4096]{1,0:T(8,128)S(1)}, u32[]{:S(2)}, u32[]{:S(2)}) %collective-permute-start.5) | collective-permute-done | bytes 131104 | tf_op jit(solution)/shard_map/ppermute | solution.py:32
  87.4 5.6 %all_gather.7 = f32[8,8192]{1,0:T(8,128)S(1)} all-gather(f32[8,4096]{1,0:T(8,128)S(1)} %collective-permute-done.5), channel_id=1, replica_groups=mesh['sec'=2,'cpl'=2,'dom'=8] {'cpl'}, dimensions={1}, use_global_device_ids=true | all-gather | bytes 393216 | tf_op jit(solution)/shard_map/all_gather | solution.py:100
  93.0 0.8 multiply_bitcast_fusion
  93.8 0.9 copy.20
  (37 shorter events, 0.5 us)
Async XLA Ops:
  7.2 8.4 %copy-start = (bf16[1,24,128,128]{3,2,1,0:T(8,128)(2,1)S(1)}, bf16[1,24,128,128]{3,2,1,0:T(8,128)(2,1)}, u32[]{:S(2)}) copy-start(bf16[1,24,128,128]{3,2,1,0:T(8,128)(2,1)} %param.10) | copy-start | bytes 2359300
  7.2 31.0 %reduce-scatter.3.cloned.1.call-start = ((), (), s32[]{:S(2)}) async-start(), calls=%async_computation.2 | async-start | bytes 1179648 | tf_op jit(solution)/shard_map/reduce_scatter | solution.py:89
  8.5 4.6 %copy-start.5 = (s32[1,24]{1,0:T(1,128)S(1)}, s32[1,24]{1,0:T(1,128)}, u32[]{:S(2)}) copy-start(s32[1,24]{1,0:T(1,128)} %param.11) | copy-start | bytes 292
  8.5 6.3 %collective-permute-start = (bf16[24,1024]{1,0:T(8,128)(2,1)S(1)}, bf16[24,1024]{1,0:T(8,128)(2,1)S(1)}, u32[]{:S(2)}, u32[]{:S(2)}) collective-permute-start(bf16[24,1024]{1,0:T(8,128)(2,1)S(1)} %get-tuple-element.18), channel_id=1, source_target_pairs={{0,1},{1,2},{2,3},{3,4},{4,5},{5,6},{6,7},{7,0},{8,9},{9,10},{10,1... | collective-permute-start | bytes 147464 | tf_op jit(solution)/shard_map/ppermute | solution.py:17
  9.0 5.9 %collective-permute-start.1 = (bf16[24,1024]{1,0:T(8,128)(2,1)S(1)}, bf16[24,1024]{1,0:T(8,128)(2,1)S(1)}, u32[]{:S(2)}, u32[]{:S(2)}) collective-permute-start(bf16[24,1024]{1,0:T(8,128)(2,1)S(1)} %get-tuple-element.19), channel_id=1, source_target_pairs={{1,0},{2,1},{3,2},{4,3},{5,4},{6,5},{7,6},{0,7},{9,8},{10,9},{11,1... | collective-permute-start | bytes 147464 | tf_op jit(solution)/shard_map/ppermute | solution.py:20
  13.1 0.7 copy-start.6
  18.9 0.8 copy-start.4
  18.9 0.8 copy-start.7
  18.9 20.8 %copy-start.8 = (s32[1,24]{1,0:T(1,128)S(1)}, s32[1,24]{1,0:T(1,128)}, u32[]{:S(2)}) copy-start(s32[1,24]{1,0:T(1,128)} %param.15) | copy-start | bytes 292
  18.9 41.0 %copy-start.1 = (f32[1,24,8192]{2,1,0:T(8,128)S(1)}, f32[1,24,8192]{2,1,0:T(8,128)}, u32[]{:S(2)}) copy-start(f32[1,24,8192]{2,1,0:T(8,128)} %param.8) | copy-start | bytes 2359300
  18.9 63.1 %reduce-scatter.5.cloned.1.call-start = ((), (), s32[]{:S(2)}) async-start(), calls=%async_computation.3 | async-start | bytes 393216 | tf_op jit(solution)/shard_map/reduce_scatter | solution.py:98
  38.2 11.0 %collective-permute-start.2 = (f32[24,4096]{1,0:T(8,128)}, f32[24,4096]{1,0:T(8,128)S(1)}, u32[]{:S(2)}, u32[]{:S(2)}) collective-permute-start(f32[24,4096]{1,0:T(8,128)} %reduce-scatter.3.cloned.1.call-done), channel_id=1, source_target_pairs={{0,16},{16,0},{1,17},{17,1},{2,18},{18,2},{3,19},{19,3},{4,20},{20... | collective-permute-start | bytes 1179656 | tf_op jit(solution)/shard_map/ppermute | solution.py:32
  61.0 6.1 %copy-start.3 = (bf16[1,24,128,128]{3,2,1,0:T(8,128)(2,1)S(1)}, bf16[1,24,128,128]{3,2,1,0:T(8,128)(2,1)}, u32[]{:S(2)}) copy-start(bf16[1,24,128,128]{3,2,1,0:T(8,128)(2,1)} %param.13) | copy-start | bytes 2359300
  61.4 5.0 %collective-permute-start.3 = (bf16[8,1024]{1,0:T(8,128)(2,1)S(1)}, bf16[8,1024]{1,0:T(8,128)(2,1)S(1)}, u32[]{:S(2)}, u32[]{:S(2)}) collective-permute-start(bf16[8,1024]{1,0:T(8,128)(2,1)S(1)} %get-tuple-element.20), channel_id=1, source_target_pairs={{0,1},{1,2},{2,3},{3,4},{4,5},{5,6},{6,7},{7,0},{8,9},{9,10},{10,1... | collective-permute-start | bytes 49160 | tf_op jit(solution)/shard_map/ppermute | solution.py:17
  61.5 5.0 %collective-permute-start.4 = (bf16[8,1024]{1,0:T(8,128)(2,1)S(1)}, bf16[8,1024]{1,0:T(8,128)(2,1)S(1)}, u32[]{:S(2)}, u32[]{:S(2)}) collective-permute-start(bf16[8,1024]{1,0:T(8,128)(2,1)S(1)} %get-tuple-element.21), channel_id=1, source_target_pairs={{1,0},{2,1},{3,2},{4,3},{5,4},{6,5},{7,6},{0,7},{9,8},{10,9},{11,1... | collective-permute-start | bytes 49160 | tf_op jit(solution)/shard_map/ppermute | solution.py:20
  69.2 0.7 copy-start.2
  82.0 5.4 %collective-permute-start.5 = (f32[8,4096]{1,0:T(8,128)}, f32[8,4096]{1,0:T(8,128)S(1)}, u32[]{:S(2)}, u32[]{:S(2)}) collective-permute-start(f32[8,4096]{1,0:T(8,128)} %reduce-scatter.5.cloned.1.call-done), channel_id=1, source_target_pairs={{0,16},{16,0},{1,17},{17,1},{2,18},{18,2},{3,19},{19,3},{4,20},{20... | collective-permute-start | bytes 393224 | tf_op jit(solution)/shard_map/ppermute | solution.py:32
Sparse Core Ops, SparseCore 0:
  19.0 19.1 reduce-scatter.2
  70.0 11.9 reduce-scatter.4
where the time goes:
time: 102 us
  waiting for transfers between devices  46.7 us (46%)
  blocking collectives  16.3 us (16%)
  between operations  14.2 us (14%)
  starting transfers between devices  11.2 us (11%)
  other arithmetic  6.91 us (7%)
  local copies, waits for them, and re-layouts  5.51 us (5%)
    reduce_scatter x1, waiting for transfers between devices, body(): lax.psum_scatter(partial_sum, 'cpl', scatter_dimension=1, tiled=True)  18.5 us
    ppermute x2, waiting for transfers between devices, swapped(): return lax.ppermute(block, axis, route)  13.5 us
    reduce_scatter x1, waiting for transfers between devices, body(): lax.psum_scatter(flux_part, 'cpl', scatter_dimension=1, tiled=True)  12.1 us
    all_gather x1, blocking collectives, body(): received = lax.all_gather(crossed, 'cpl', axis=1, tiled=True)  10.6 us
    ppermute x2, starting transfers between devices, extended_2(): lax.ppermute(lax.slice_in_dim(block, 0, width, axis=dim), axis, backward)  7.63 us
    all_gather x1, blocking collectives, body(): flux_back = lax.all_gather(flux_crossed, 'cpl', axis=1, tiled=True)  5.63 us
    scatter-add x2, other arithmetic, remap_local(): jnp.zeros((row_count, local_blocks, TILE), jnp.float32).at[:, target]  3.63 us
    unnamed x19, local copies, waits for them, and re-layouts  2.92 us
  transfers between devices with their start and end apart: 8, of which 6 were waited for; matrix products, arithmetic and copies ran while one was open for 0% of the time, Pallas kernels for 0%

commit v1 on v0

v1 whole, which is shorter than its diff:
```python
import functools

import jax
import jax.numpy as jnp
from jax import lax
from jax.experimental import pallas as pl
from jax.experimental.pallas import tpu as pltpu
from jax.sharding import PartitionSpec as P

TILE = 128
BULK_ITERS = 3
RIM = 8
CRIT = 8
MESH = pl.DeviceIdType.MESH


def bulk_flux(atmos, ocean, wet_frac):
    wind_u = atmos[0] - ocean[0]
    wind_v = atmos[1] - ocean[1]
    square = wind_u * wind_u + wind_v * wind_v + 0.5
    wind_speed = jnp.sqrt(square)
    temp_diff = atmos[2] - ocean[2]
    humid_diff = atmos[3] - 0.5 * ocean[3]
    neutral = 1.0 + 0.5 * jnp.tanh(atmos[4] + ocean[4])
    richardson = 2.0 * temp_diff / square
    drag_coef = neutral
    for _ in range(BULK_ITERS):
        drag_coef = neutral * (1.0 + 0.8 * jnp.tanh(-richardson * drag_coef))
    transfer = drag_coef * wind_speed
    rows = [
        0.5 * transfer * wind_u,
        0.5 * transfer * wind_v,
        0.5 * transfer * temp_diff,
        0.5 * transfer * humid_diff,
        atmos[5] * (1.0 - 0.3 * jnp.tanh(ocean[5])),
        atmos[6] - 0.5 * ocean[2],
        atmos[7] - 0.15 * transfer * humid_diff,
        0.5 * jnp.sqrt(drag_coef) * wind_speed,
    ]
    return [row * wet_frac for row in rows]


def kernel(
    sizes,
    ssrc, stgt, fsrc, ftgt,
    fields_hbm, wet_hbm, wstate_hbm, wflux_hbm,
    deliv_hbm, flux_hbm,
    xin, xext, wet, wstate, wflux, pcrit, prest, fbuf, fext, dout, fout, own_stage, got_stage,
    xsend, xrecv, fsend, frecv,
    tab, tab_recv, tab_own_s, tab_s,
    asend, arecv, bsend, brecv, csend, crecv, afull, cfull,
    load_sem, tabcopy_sem, out_sem,
    xs_sem, xr_sem, fs_sem, fr_sem,
    ts_sem, tr_sem, as_sem, ar_sem, bs_sem, br_sem, cs_sem, cr_sem,
):
    rows, nblk, tpd, ncpl, ndom = sizes
    rest = rows - CRIT
    edge = RIM * TILE
    cells = nblk * TILE
    sec = lax.axis_index("sec")
    cpl = lax.axis_index("cpl")
    dom = lax.axis_index("dom")
    right = lax.rem(dom + 1, ndom)
    left = lax.rem(dom + ndom - 1, ndom)
    other = 1 - sec

    loads = [
        pltpu.make_async_copy(fields_hbm.at[0, :, pl.ds(0, edge)], xin.at[:, pl.ds(0, edge)], load_sem.at[0]),
        pltpu.make_async_copy(fields_hbm.at[0, :, pl.ds(cells - edge, edge)], xin.at[:, pl.ds(cells - edge, edge)], load_sem.at[1]),
        pltpu.make_async_copy(fields_hbm.at[0, :, pl.ds(edge, cells - 2 * edge)], xin.at[:, pl.ds(edge, cells - 2 * edge)], load_sem.at[2]),
        pltpu.make_async_copy(wstate_hbm.at[0], wstate, load_sem.at[3]),
        pltpu.make_async_copy(wflux_hbm.at[0], wflux, load_sem.at[4]),
        pltpu.make_async_copy(wet_hbm, wet, load_sem.at[5]),
    ]
    for load in loads:
        load.start()

    barrier = pltpu.get_barrier_semaphore()
    for neighbour in (left, right):
        pl.semaphore_signal(barrier, inc=1, device_id={"dom": neighbour}, device_id_type=MESH)
    partners = [lax.rem(cpl + step, ncpl) for step in range(ncpl)]
    for partner in partners:
        pl.semaphore_signal(barrier, inc=1, device_id={"sec": other, "cpl": partner}, device_id_type=MESH)

    lane = lax.broadcasted_iota(jnp.int32, (8, 2 * nblk), 1)
    sub = lax.broadcasted_iota(jnp.int32, (8, 2 * nblk), 0)
    last = jnp.full((8, 2 * nblk), tpd, jnp.int32)
    prev = jnp.full((8, 2 * nblk), tpd, jnp.int32)
    trow = jnp.full((8, 2 * nblk), -1, jnp.int32)

    def mark(j, carry):
        last, trow = carry
        a = stgt[0, j]
        b = ftgt[0, j] + nblk
        last = jnp.where((lane == a) | (lane == b), j, last)
        trow = jnp.where(lane == j, a, trow)
        trow = jnp.where(lane == j + nblk, b, trow)
        return last, trow

    last, trow = lax.fori_loop(0, tpd, mark, (last, trow), unroll=True)

    def link(j, prev):
        a = stgt[0, j]
        b = ftgt[0, j] + nblk
        prev = jnp.where((trow == a) & (lane > j), j, prev)
        return jnp.where((trow == b) & (lane > j + nblk), j, prev)

    prev = lax.fori_loop(0, tpd, link, prev, unroll=True)
    tab[...] = jnp.where(sub == 0, last, prev)
    own_tab = pltpu.make_async_copy(tab, tab_own_s, tabcopy_sem.at[ncpl])
    own_tab.start()

    pcrit[tpd] = jnp.zeros((CRIT, TILE), jnp.float32)
    prest[tpd] = jnp.zeros((rest, TILE), jnp.float32)
    fbuf[tpd] = jnp.zeros((CRIT, TILE), jnp.float32)
    for k in range(ncpl):
        afull[k, tpd] = jnp.zeros((CRIT, TILE), jnp.float32)
        cfull[k, tpd] = jnp.zeros((CRIT, TILE), jnp.float32)
        brecv[k, tpd] = jnp.zeros((rest, TILE), jnp.bfloat16)

    for side in range(2):
        loads[side].wait()
        start = 0 if side == 0 else cells - edge
        for pair in range(RIM // 2):
            at = start + 2 * pair * TILE
            both = jnp.concatenate([xin[:, at : at + TILE], xin[:, at + TILE : at + 2 * TILE]], axis=0)
            xsend[side, 2 * rows * pair : 2 * rows * (pair + 1), :] = both.astype(jnp.bfloat16)

    pl.semaphore_wait(barrier, 2 + ncpl)

    def halo(send, recv, ssem, rsem, side):
        return pltpu.make_async_remote_copy(
            src_ref=send.at[side], dst_ref=recv.at[side], send_sem=ssem.at[side], recv_sem=rsem.at[side],
            device_id={"dom": left if side == 0 else right}, device_id_type=MESH,
        )

    def cross(src, dst, ssem, rsem, step):
        return pltpu.make_async_remote_copy(
            src_ref=src, dst_ref=dst(cpl), send_sem=ssem.at[step], recv_sem=rsem.at[cpl],
            device_id={"sec": other, "cpl": partners[step]}, device_id_type=MESH,
        )

    def arrived(src, dst, ssem, rsem, k):
        pltpu.make_async_remote_copy(
            src_ref=src, dst_ref=dst(k), send_sem=ssem.at[0], recv_sem=rsem.at[k],
            device_id={"sec": other}, device_id_type=MESH,
        ).wait_recv()

    xhalos = [halo(xsend, xrecv, xs_sem, xr_sem, side) for side in range(2)]
    for copy in xhalos:
        copy.start()
    tabs = [cross(tab, lambda k: tab_recv.at[k], ts_sem, tr_sem, step) for step in range(ncpl)]
    for copy in tabs:
        copy.start()

    own_tab.wait()
    loads[2].wait()

    def extend(group, carry):
        for i in range(8):
            b = group * 8 + i
            xext[RIM + b] = xin[:, pl.ds(pl.multiple_of(b * TILE, TILE), TILE)]
        return carry

    lax.fori_loop(0, nblk // 8, extend, 0)
    loads[3].wait()
    for side in range(2):
        xhalos[side].wait_recv()
        start = RIM + nblk if side == 0 else 0
        for pair in range(RIM // 2):
            at = start + 2 * pair
            both = xrecv[side, 2 * rows * pair : 2 * rows * (pair + 1), :].astype(jnp.float32)
            xext[at] = both[:rows]
            xext[at + 1] = both[rows:]

    def state_product(j, carry):
        piece = xext[ssrc[0, j]].astype(jnp.bfloat16)
        product = jnp.dot(piece, wstate[j], preferred_element_type=jnp.float32)
        pcrit[j] = product[:CRIT]
        prest[j] = product[CRIT:]
        return carry

    lax.fori_loop(0, tpd, state_product, 0, unroll=True)

    def chain_crit(j, carry):
        pcrit[j] = pcrit[j] + pcrit[tab_own_s[1, j]]
        return carry

    lax.fori_loop(0, tpd, chain_crit, 0, unroll=True)
    for pair in range(tpd // 2):
        both = jnp.concatenate([pcrit[2 * pair], pcrit[2 * pair + 1]], axis=0)
        asend[2 * CRIT * pair : 2 * CRIT * (pair + 1), :] = both.astype(jnp.bfloat16)
    acopies = [cross(asend, lambda k: arecv.at[k], as_sem, ar_sem, step) for step in range(ncpl)]
    for copy in reversed(acopies):
        copy.start()

    def chain_rest(j, carry):
        total = prest[j] + prest[tab_own_s[1, j]]
        prest[j] = total
        bsend[j] = total.astype(jnp.bfloat16)
        return carry

    lax.fori_loop(0, tpd, chain_rest, 0, unroll=True)
    bdst = lambda k: brecv.at[k, pl.ds(0, tpd)]
    bcopies = [cross(bsend, bdst, bs_sem, br_sem, step) for step in range(ncpl)]
    for copy in reversed(bcopies):
        copy.start()

    tabcopies = []
    for k in range(ncpl):
        arrived(tab, lambda k: tab_recv.at[k], ts_sem, tr_sem, k)
        copy = pltpu.make_async_copy(tab_recv.at[k], tab_s.at[k], tabcopy_sem.at[k])
        copy.start()
        tabcopies.append(copy)
    for copy in tabcopies:
        copy.wait()
    loads[5].wait()

    for k in range(ncpl):
        arrived(asend, lambda k: arecv.at[k], as_sem, ar_sem, k)
        for pair in range(tpd // 2):
            both = arecv[k, 2 * CRIT * pair : 2 * CRIT * (pair + 1), :].astype(jnp.float32)
            afull[k, 2 * pair] = both[:CRIT]
            afull[k, 2 * pair + 1] = both[CRIT:]

    first_sec = sec == 0

    def solve(group):
        for i in range(8):
            b = group * 8 + i
            got = afull[0, tab_s[0, 0, b]]
            for k in range(1, ncpl):
                got = got + afull[k, tab_s[k, 0, b]]
            at = pl.multiple_of(b * TILE, TILE)
            dout[:CRIT, pl.ds(at, TILE)] = got
            got_stage[CRIT * i : CRIT * (i + 1), :] = got
            own_stage[CRIT * i : CRIT * (i + 1), :] = xin[:CRIT, pl.ds(at, TILE)]
        atmos, ocean = [], []
        for r in range(CRIT):
            mine = own_stage[pl.ds(r, 8, stride=CRIT), :]
            got = got_stage[pl.ds(r, 8, stride=CRIT), :]
            atmos.append(jnp.where(first_sec, mine, got))
            ocean.append(jnp.where(first_sec, got, mine))
        wet_frac = wet[pl.ds(pl.multiple_of(group * 8, 8), 8), :].astype(jnp.float32)
        result = bulk_flux(atmos, ocean, wet_frac)
        for r in range(CRIT):
            got_stage[pl.ds(r, 8, stride=CRIT), :] = result[r]
        for i in range(8):
            fext[RIM + group * 8 + i] = got_stage[CRIT * i : CRIT * (i + 1), :]

    fhalos = [halo(fsend, frecv, fs_sem, fr_sem, side) for side in range(2)]
    for side, group in ((0, 0), (1, nblk // 8 - 1)):
        solve(group)
        fsend[side] = got_stage[...].astype(jnp.bfloat16)
        fhalos[side].start()

    def middle(group, carry):
        solve(group)
        return carry

    lax.fori_loop(1, nblk // 8 - 1, middle, 0)

    loads[4].wait()
    for side in range(2):
        fhalos[side].wait_recv()
        base = RIM + nblk if side == 0 else 0
        for pair in range(RIM // 2):
            both = frecv[side, 2 * CRIT * pair : 2 * CRIT * (pair + 1), :].astype(jnp.float32)
            fext[base + 2 * pair] = both[:CRIT]
            fext[base + 2 * pair + 1] = both[CRIT:]

    def flux_product(j, carry):
        piece = fext[fsrc[0, j]].astype(jnp.bfloat16)
        fbuf[j] = jnp.dot(piece, wflux[j], preferred_element_type=jnp.float32)
        return carry

    lax.fori_loop(0, tpd, flux_product, 0, unroll=True)

    def chain_flux(j, carry):
        fbuf[j] = fbuf[j] + fbuf[tab_own_s[1, j + nblk]]
        return carry

    lax.fori_loop(0, tpd, chain_flux, 0, unroll=True)
    for pair in range(tpd // 2):
        both = jnp.concatenate([fbuf[2 * pair], fbuf[2 * pair + 1]], axis=0)
        csend[2 * CRIT * pair : 2 * CRIT * (pair + 1), :] = both.astype(jnp.bfloat16)
    ccopies = [cross(csend, lambda k: crecv.at[k], cs_sem, cr_sem, step) for step in range(ncpl)]
    for copy in reversed(ccopies):
        copy.start()

    for k in range(ncpl):
        arrived(bsend, bdst, bs_sem, br_sem, k)

    def place(group, carry):
        for i in range(8):
            b = group * 8 + i
            got = brecv[0, tab_s[0, 0, b]].astype(jnp.float32)
            for k in range(1, ncpl):
                got = got + brecv[k, tab_s[k, 0, b]].astype(jnp.float32)
            dout[CRIT:, pl.ds(pl.multiple_of(b * TILE, TILE), TILE)] = got
        return carry

    lax.fori_loop(0, nblk // 8, place, 0)
    deliver = pltpu.make_async_copy(dout, deliv_hbm, out_sem.at[0])
    deliver.start()

    for k in range(ncpl):
        arrived(csend, lambda k: crecv.at[k], cs_sem, cr_sem, k)
        for pair in range(tpd // 2):
            both = crecv[k, 2 * CRIT * pair : 2 * CRIT * (pair + 1), :].astype(jnp.float32)
            cfull[k, 2 * pair] = both[:CRIT]
            cfull[k, 2 * pair + 1] = both[CRIT:]

    def merge(group, carry):
        wet_frac = wet[pl.ds(pl.multiple_of(group * 8, 8), 8), :].astype(jnp.float32)
        for i in range(8):
            b = group * 8 + i
            back = cfull[0, tab_s[0, 0, b + nblk]]
            for k in range(1, ncpl):
                back = back + cfull[k, tab_s[k, 0, b + nblk]]
            own = fext[RIM + b]
            fout[:, pl.ds(pl.multiple_of(b * TILE, TILE), TILE)] = 0.5 * (own + wet_frac[i : i + 1] * back)
        return carry

    lax.fori_loop(0, nblk // 8, merge, 0)
    store = pltpu.make_async_copy(fout, flux_hbm, out_sem.at[1])
    store.start()

    for copy in xhalos + tabs + acopies + bcopies + fhalos + ccopies:
        copy.wait_send()
    deliver.wait()
    store.wait()


def body(ncpl, ndom, fields, wet_mask, wstate, ssrc, stgt, wflux, fsrc, ftgt):
    rows, cells = fields.shape[1:]
    nblk = cells // TILE
    tpd = wstate.shape[1]
    rest = rows - CRIT
    f32, bf16, i32 = jnp.float32, jnp.bfloat16, jnp.int32
    vmem, dma = pltpu.VMEM, pltpu.SemaphoreType.DMA
    smem_spec = pl.BlockSpec(memory_space=pltpu.SMEM)
    any_spec = pl.BlockSpec(memory_space=pl.ANY)
    delivered, fluxes = pl.pallas_call(
        functools.partial(kernel, (rows, nblk, tpd, ncpl, ndom)),
        out_shape=(
            jax.ShapeDtypeStruct((rows, cells), f32),
            jax.ShapeDtypeStruct((CRIT, cells), f32),
        ),
        in_specs=[smem_spec] * 4 + [any_spec] * 4,
        out_specs=(any_spec, any_spec),
        scratch_shapes=[
            vmem((rows, cells), f32),
            vmem((nblk + 2 * RIM, rows, TILE), f32),
            vmem((nblk, TILE), i32),
            vmem((tpd, TILE, TILE), bf16),
            vmem((tpd, TILE, TILE), bf16),
            vmem((tpd + 1, CRIT, TILE), f32),
            vmem((tpd + 1, rest, TILE), f32),
            vmem((tpd + 1, CRIT, TILE), f32),
            vmem((nblk + 2 * RIM, CRIT, TILE), f32),
            vmem((rows, cells), f32),
            vmem((CRIT, cells), f32),
            vmem((8 * CRIT, TILE), f32),
            vmem((8 * CRIT, TILE), f32),
            vmem((2, RIM * rows, TILE), bf16),
            vmem((2, RIM * rows, TILE), bf16),
            vmem((2, RIM * CRIT, TILE), bf16),
            vmem((2, RIM * CRIT, TILE), bf16),
            vmem((8, 2 * nblk), i32),
            vmem((ncpl, 8, 2 * nblk), i32),
            pltpu.SMEM((8, 2 * nblk), i32),
            pltpu.SMEM((ncpl, 8, 2 * nblk), i32),
            vmem((tpd * CRIT, TILE), bf16),
            vmem((ncpl, tpd * CRIT, TILE), bf16),
            vmem((tpd, rest, TILE), bf16),
            vmem((ncpl, tpd + 1, rest, TILE), bf16),
            vmem((tpd * CRIT, TILE), bf16),
            vmem((ncpl, tpd * CRIT, TILE), bf16),
            vmem((ncpl, tpd + 1, CRIT, TILE), f32),
            vmem((ncpl, tpd + 1, CRIT, TILE), f32),
            dma((6,)), dma((ncpl + 1,)), dma((2,)),
            dma((2,)), dma((2,)), dma((2,)), dma((2,)),
            dma((ncpl,)), dma((ncpl,)), dma((ncpl,)), dma((ncpl,)),
            dma((ncpl,)), dma((ncpl,)), dma((ncpl,)), dma((ncpl,)),
        ],
        compiler_params=pltpu.CompilerParams(
            collective_id=0, has_side_effects=True, vmem_limit_bytes=40 * 1024 * 1024
        ),
    )(ssrc, stgt, fsrc, ftgt, fields, wet_mask.reshape(nblk, TILE), wstate, wflux)
    return delivered[None], fluxes[None]


def solution(mesh):
    tile_spec = P("sec", ("cpl", "dom"), None, None)
    index_spec = P("sec", ("cpl", "dom"))
    return jax.shard_map(
        functools.partial(body, mesh.shape["cpl"], mesh.shape["dom"]),
        mesh=mesh,
        in_specs=(
            P("sec", None, "dom"), P("sec", "dom"),
            tile_spec, index_spec, index_spec,
            tile_spec, index_spec, index_spec,
        ),
        out_specs=(P("sec", None, "dom"), P("sec", None, "dom")),
        check_vma=False,
    )
```

time: 102 us -> 29.9 us (0.29)
  waiting for transfers between devices: 46.7 us -> 0 us
  Pallas kernels: 0 us -> 21.8 us
  blocking collectives: 16.3 us -> 0 us
  between operations: 14.2 us -> 0.67 us
  starting transfers between devices: 11.2 us -> 0 us
  other arithmetic: 6.91 us -> 0 us
  local copies, waits for them, and re-layouts: 5.51 us -> 7.06 us
    reduce_scatter x2 -> x0, waiting for transfers between devices: 30.6 us -> none  [the longest x1 18.5 us: body(): lax.psum_scatter(partial_sum, 'cpl', scatter_dimension=1, tiled=True)]
    pallas_call x0 -> x1, Pallas kernels: none -> 21.8 us  [body(): pl.pallas_call(functools.partial(kernel, (rows, nblk, tpd, ncpl, ndom)),...]
    all_gather x2 -> x0, blocking collectives: 16.3 us -> none  [the longest x1 10.6 us: body(): received = lax.all_gather(crossed, 'cpl', axis=1, tiled=True)]
    ppermute x6 -> x0, waiting for transfers between devices: 16 us -> none  [the longest x2 13.5 us: swapped(): return lax.ppermute(block, axis, route)]
    ppermute x6 -> x0, starting transfers between devices: 11.1 us -> none  [the longest x2 7.63 us: extended_2(): lax.ppermute(lax.slice_in_dim(block, 0, width, axis=dim), axis, backward)]
    unnamed x19 -> x18, local copies, waits for them, and re-layouts: 2.92 us -> 7.06 us
    scatter-add x2 -> x0, other arithmetic: 3.63 us -> none  [remap_local(): jnp.zeros((row_count, local_blocks, TILE), jnp.float32).at[:, target]]
    convert_element_type x3 -> x0, other arithmetic: 1.3 us -> none  [the longest x1 1.24 us: body(): own_fields.astype(jnp.bfloat16)]
  transfers between devices with their start and end apart: 8 -> 0, of which waited for: 6 -> 0; matrix products, arithmetic and copies ran while one was open for 0% -> 0% of each run, Pallas kernels for 0% -> 0%
where the time goes in v1:
time: 29.9 us; the launch traced here: 29.6 us
  Pallas kernels  21.8 us (73%)
  local copies, waits for them, and re-layouts  7.06 us (24%)
  between operations  0.67 us (2%)
    pallas_call x1, Pallas kernels, body(): pl.pallas_call(functools.partial(kernel, (rows, nblk, tpd, ncpl, ndom)),...  21.8 us
    unnamed x18, local copies, waits for them, and re-layouts  7.06 us

profile of v1, /device:TPU:0, one launch (start us, length us, event | category | flops | bytes accessed | tf_op | source)
XLA Modules:
  0.0 29.6 jit_solution(224180990543058868)
XLA Ops:
  0.6 0.0 copy-start.6
  0.6 0.0 copy-start.5
  0.7 0.0 copy-start.4
  0.7 0.6 %copy-done.6 = s32[1,24]{1,0:T(1,128)S(1)} copy-done((s32[1,24]{1,0:T(1,128)S(1)}, s32[1,24]{1,0:T(1,128)}, u32[]{:S(2)}) %copy-start.6) | copy-done | bytes 120
  1.3 0.0 copy-done.5
  1.3 0.0 copy-done.4
  1.3 0.0 copy-start
  1.3 1.1 %copy-done = f32[1,24,8192]{2,1,0:T(8,128)S(1)} copy-done((f32[1,24,8192]{2,1,0:T(8,128)S(1)}, f32[1,24,8192]{2,1,0:T(8,128)}, u32[]{:S(2)}) %copy-start) | copy-done | bytes 786456
  2.5 0.0 copy-start.1
  2.5 1.1 %copy-done.1 = bf16[1,24,128,128]{3,2,1,0:T(8,128)(2,1)S(1)} copy-done((bf16[1,24,128,128]{3,2,1,0:T(8,128)(2,1)S(1)}, bf16[1,24,128,128]{3,2,1,0:T(8,128)(2,1)}, u32[]{:S(2)}) %copy-start.1) | copy-done | bytes 786456
  3.6 0.0 copy-start.2
  3.6 1.1 %copy-done.2 = bf16[1,24,128,128]{3,2,1,0:T(8,128)(2,1)S(1)} copy-done((bf16[1,24,128,128]{3,2,1,0:T(8,128)(2,1)S(1)}, bf16[1,24,128,128]{3,2,1,0:T(8,128)(2,1)}, u32[]{:S(2)}) %copy-start.2) | copy-done | bytes 786456
  4.7 0.0 copy-start.3
  4.7 0.8 %copy-done.3 = s32[1,8192]{1,0:T(1,128)S(1)} copy-done((s32[1,8192]{1,0:T(1,128)S(1)}, s32[1,8192]{1,0:T(1,128)}, u32[]{:S(2)}) %copy-start.3) | copy-done | bytes 32792
  5.5 0.0 copy-start.7
  5.5 0.7 %copy-done.7 = s32[1,24]{1,0:T(1,128)S(1)} copy-done((s32[1,24]{1,0:T(1,128)S(1)}, s32[1,24]{1,0:T(1,128)}, u32[]{:S(2)}) %copy-start.7) | copy-done | bytes 120
  6.1 21.8 %shard_map.95 = (f32[24,8192]{1,0:T(8,128)S(1)}, f32[8,8192]{1,0:T(8,128)S(1)}) custom-call(s32[1,24]{1,0:T(1,128)S(1)} %copy-done.4, s32[1,24]{1,0:T(1,128)S(1)} %copy-done.5, s32[1,24]{1,0:T(1,128)S(1)} %copy-done.6, s32[1,24]{1,0:T(1,128)S(1)} %copy-done.7, f32[1,24,8192]{2,1,0:T(8,128)S(1)} %copy-done, s32[64,128]{1,0:T(8,128)S(1)} %bitcast.5, ...), custom_call_target="tpu_custom_call" | custom-call | tf_op jit(solution)/shard_map/pallas_call | solution.py:344
  28.0 0.9 %copy.12 = f32[1,24,8192]{2,1,0:T(8,128)} copy(f32[1,24,8192]{2,1,0:T(8,128)S(1)} %bitcast.3) | data formatting | bytes 1572864
  28.9 0.7 %copy.13 = f32[1,8,8192]{2,1,0:T(8,128)} copy(f32[1,8,8192]{2,1,0:T(8,128)S(1)} %bitcast.4) | data formatting | bytes 524288
Async XLA Ops:
  0.6 0.7 %copy-start.6 = (s32[1,24]{1,0:T(1,128)S(1)}, s32[1,24]{1,0:T(1,128)}, u32[]{:S(2)}) copy-start(s32[1,24]{1,0:T(1,128)} %fsrc.1) | copy-start | bytes 292
  0.6 0.7 %copy-start.5 = (s32[1,24]{1,0:T(1,128)S(1)}, s32[1,24]{1,0:T(1,128)}, u32[]{:S(2)}) copy-start(s32[1,24]{1,0:T(1,128)} %stgt.1) | copy-start | bytes 292
  0.7 0.7 %copy-start.4 = (s32[1,24]{1,0:T(1,128)S(1)}, s32[1,24]{1,0:T(1,128)}, u32[]{:S(2)}) copy-start(s32[1,24]{1,0:T(1,128)} %ssrc.1) | copy-start | bytes 292
  1.3 1.1 %copy-start = (f32[1,24,8192]{2,1,0:T(8,128)S(1)}, f32[1,24,8192]{2,1,0:T(8,128)}, u32[]{:S(2)}) copy-start(f32[1,24,8192]{2,1,0:T(8,128)} %fields_hbm.1) | copy-start | bytes 2359300
  2.5 1.1 %copy-start.1 = (bf16[1,24,128,128]{3,2,1,0:T(8,128)(2,1)S(1)}, bf16[1,24,128,128]{3,2,1,0:T(8,128)(2,1)}, u32[]{:S(2)}) copy-start(bf16[1,24,128,128]{3,2,1,0:T(8,128)(2,1)} %wstate_hbm.1) | copy-start | bytes 2359300
  3.6 1.1 %copy-start.2 = (bf16[1,24,128,128]{3,2,1,0:T(8,128)(2,1)S(1)}, bf16[1,24,128,128]{3,2,1,0:T(8,128)(2,1)}, u32[]{:S(2)}) copy-start(bf16[1,24,128,128]{3,2,1,0:T(8,128)(2,1)} %wflux_hbm.1) | copy-start | bytes 2359300
  4.7 0.8 %copy-start.3 = (s32[1,8192]{1,0:T(1,128)S(1)}, s32[1,8192]{1,0:T(1,128)}, u32[]{:S(2)}) copy-start(s32[1,8192]{1,0:T(1,128)} %param.9) | copy-start | bytes 98308
  5.5 0.7 %copy-start.7 = (s32[1,24]{1,0:T(1,128)S(1)}, s32[1,24]{1,0:T(1,128)}, u32[]{:S(2)}) copy-start(s32[1,24]{1,0:T(1,128)} %ftgt.1) | copy-start | bytes 292

commit v2 on v1

--- a/solution.py
+++ b/solution.py
@@ -42,9 +42,10 @@
 
 def kernel(
     sizes,
-    ssrc, stgt, fsrc, ftgt,
+    ssrc_hbm, stgt_hbm, fsrc_hbm, ftgt_hbm,
     fields_hbm, wet_hbm, wstate_hbm, wflux_hbm,
     deliv_hbm, flux_hbm,
+    ssrc, stgt, fsrc, ftgt,
     xin, xext, wet, wstate, wflux, pcrit, prest, fbuf, fext, dout, fout, own_stage, got_stage,
     xsend, xrecv, fsend, frecv,
     tab, tab_recv, tab_own_s, tab_s,
@@ -64,6 +65,12 @@
     left = lax.rem(dom + ndom - 1, ndom)
     other = 1 - sec
 
+    indices = [
+        pltpu.make_async_copy(src, dst, load_sem.at[6 + i])
+        for i, (src, dst) in enumerate(((stgt_hbm, stgt), (ftgt_hbm, ftgt), (ssrc_hbm, ssrc), (fsrc_hbm, fsrc)))
+    ]
+    for load in indices:
+        load.start()
     loads = [
         pltpu.make_async_copy(fields_hbm.at[0, :, pl.ds(0, edge)], xin.at[:, pl.ds(0, edge)], load_sem.at[0]),
         pltpu.make_async_copy(fields_hbm.at[0, :, pl.ds(cells - edge, edge)], xin.at[:, pl.ds(cells - edge, edge)], load_sem.at[1]),
@@ -87,6 +94,9 @@
     last = jnp.full((8, 2 * nblk), tpd, jnp.int32)
     prev = jnp.full((8, 2 * nblk), tpd, jnp.int32)
     trow = jnp.full((8, 2 * nblk), -1, jnp.int32)
+
+    for load in indices:
+        load.wait()
 
     def mark(j, carry):
         last, trow = carry
@@ -339,17 +349,17 @@
     rest = rows - CRIT
     f32, bf16, i32 = jnp.float32, jnp.bfloat16, jnp.int32
     vmem, dma = pltpu.VMEM, pltpu.SemaphoreType.DMA
-    smem_spec = pl.BlockSpec(memory_space=pltpu.SMEM)
-    any_spec = pl.BlockSpec(memory_space=pl.ANY)
+    hbm_spec = pl.BlockSpec(memory_space=pltpu.HBM)
     delivered, fluxes = pl.pallas_call(
         functools.partial(kernel, (rows, nblk, tpd, ncpl, ndom)),
         out_shape=(
             jax.ShapeDtypeStruct((rows, cells), f32),
             jax.ShapeDtypeStruct((CRIT, cells), f32),
         ),
-        in_specs=[smem_spec] * 4 + [any_spec] * 4,
-        out_specs=(any_spec, any_spec),
-        scratch_shapes=[
+        in_specs=[hbm_spec] * 8,
+        out_specs=(hbm_spec, hbm_spec),
+        scratch_shapes=[pltpu.SMEM((1, tpd), i32)] * 4
+        + [
             vmem((rows, cells), f32),
             vmem((nblk + 2 * RIM, rows, TILE), f32),
             vmem((nblk, TILE), i32),
@@ -379,13 +389,13 @@
             vmem((ncpl, tpd * CRIT, TILE), bf16),
             vmem((ncpl, tpd + 1, CRIT, TILE), f32),
             vmem((ncpl, tpd + 1, CRIT, TILE), f32),
-            dma((6,)), dma((ncpl + 1,)), dma((2,)),
+            dma((10,)), dma((ncpl + 1,)), dma((2,)),
             dma((2,)), dma((2,)), dma((2,)), dma((2,)),
             dma((ncpl,)), dma((ncpl,)), dma((ncpl,)), dma((ncpl,)),
             dma((ncpl,)), dma((ncpl,)), dma((ncpl,)), dma((ncpl,)),
         ],
         compiler_params=pltpu.CompilerParams(
-            collective_id=0, has_side_effects=True, vmem_limit_bytes=40 * 1024 * 1024
+            collective_id=0, has_side_effects=True, vmem_limit_bytes=63 * 1024 * 1024
         ),
     )(ssrc, stgt, fsrc, ftgt, fields, wet_mask.reshape(nblk, TILE), wstate, wflux)
     return delivered[None], fluxes[None]

time: 29.9 us -> 25.3 us (0.85)
  local copies, waits for them, and re-layouts: 7.06 us -> 2.81 us
    unnamed x18 -> x4, local copies, waits for them, and re-layouts: 7.06 us -> 2.81 us
where the time goes in v2:
time: 25.3 us; the launch traced here: 25.2 us
  Pallas kernels  21.7 us (86%)
  local copies, waits for them, and re-layouts  2.81 us (11%)
  between operations  0.65 us (3%)
    pallas_call x1, Pallas kernels, body(): pl.pallas_call(functools.partial(kernel, (rows, nblk, tpd, ncpl, ndom)),...  21.7 us
    unnamed x4, local copies, waits for them, and re-layouts  2.81 us

profile of v2, /device:TPU:0, one launch (start us, length us, event | category | flops | bytes accessed | tf_op | source)
XLA Modules:
  0.0 25.2 jit_solution(18348528776553044188)
XLA Ops:
  0.6 21.7 %shard_map.95 = (f32[24,8192]{1,0:T(8,128)}, f32[8,8192]{1,0:T(8,128)}) custom-call(s32[1,24]{1,0:T(1,128)} %ssrc_hbm.1, s32[1,24]{1,0:T(1,128)} %stgt_hbm.1, s32[1,24]{1,0:T(1,128)} %fsrc_hbm.1, s32[1,24]{1,0:T(1,128)} %ftgt_hbm.1, f32[1,24,8192]{2,1,0:T(8,128)} %fields_hbm.1, s32[64,128]{1,0:T(8,128)} %bitcast.5, bf16[1,24,128,128]{3,2,1,0:T(8,128)(2,1)} %wstate_hbm.1, ...), custom_call_target="tpu_custom_call" | custom-call | tf_op jit(solution)/shard_map/pallas_call | solution.py:353
  22.4 0.0 copy-start
  22.4 2.1 %copy.12 = f32[1,24,8192]{2,1,0:T(8,128)} copy(f32[1,24,8192]{2,1,0:T(8,128)} %bitcast.3) | data formatting | bytes 1572864
  24.5 0.0 copy-done
  24.5 0.7 %copy.13 = f32[1,8,8192]{2,1,0:T(8,128)} copy(f32[1,8,8192]{2,1,0:T(8,128)S(1)} %bitcast.4) | data formatting | bytes 524288
Async XLA Ops:
  22.4 2.1 %copy-start = (f32[8,8192]{1,0:T(8,128)S(1)}, f32[8,8192]{1,0:T(8,128)}, u32[]{:S(2)}) copy-start(f32[8,8192]{1,0:T(8,128)} %get-tuple-element.5) | copy-start | bytes 786436

commit v3 on v2

--- a/solution.py
+++ b/solution.py
@@ -46,12 +46,12 @@
     fields_hbm, wet_hbm, wstate_hbm, wflux_hbm,
     deliv_hbm, flux_hbm,
     ssrc, stgt, fsrc, ftgt,
-    xin, xext, wet, wstate, wflux, pcrit, prest, fbuf, fext, dout, fout, own_stage, got_stage,
+    xin, xcrit, xrest, wet, wstate, wflux, pcrit, prest, fbuf, fext, dout, fout, own_stage, got_stage,
     xsend, xrecv, fsend, frecv,
     tab, tab_recv, tab_own_s, tab_s,
     asend, arecv, bsend, brecv, csend, crecv, afull, cfull,
     load_sem, tabcopy_sem, out_sem,
-    xs_sem, xr_sem, fs_sem, fr_sem,
+    xs_sem, xr_sem, ys_sem, yr_sem, fs_sem, fr_sem,
     ts_sem, tr_sem, as_sem, ar_sem, bs_sem, br_sem, cs_sem, cr_sem,
 ):
     rows, nblk, tpd, ncpl, ndom = sizes
@@ -88,6 +88,8 @@
     partners = [lax.rem(cpl + step, ncpl) for step in range(ncpl)]
     for partner in partners:
         pl.semaphore_signal(barrier, inc=1, device_id={"sec": other, "cpl": partner}, device_id_type=MESH)
+    for partner in partners[1:]:
+        pl.semaphore_signal(barrier, inc=1, device_id={"cpl": partner}, device_id_type=MESH)
 
     lane = lax.broadcasted_iota(jnp.int32, (8, 2 * nblk), 1)
     sub = lax.broadcasted_iota(jnp.int32, (8, 2 * nblk), 0)
@@ -128,15 +130,29 @@
         cfull[k, tpd] = jnp.zeros((CRIT, TILE), jnp.float32)
         brecv[k, tpd] = jnp.zeros((rest, TILE), jnp.bfloat16)
 
-    for side in range(2):
+    def extend(b):
+        at = b * TILE if isinstance(b, int) else pl.multiple_of(b * TILE, TILE)
+        xcrit[RIM + b] = xin[:CRIT, pl.ds(at, TILE)]
+        xrest[RIM + b] = xin[CRIT:, pl.ds(at, TILE)].astype(jnp.bfloat16)
+
+    def pack(send, side, ext, start):
+        for pair in range(RIM // 2):
+            both = jnp.concatenate([ext[start + 2 * pair], ext[start + 2 * pair + 1]], axis=0)
+            send[side, 2 * CRIT * pair : 2 * CRIT * (pair + 1), :] = both.astype(jnp.bfloat16)
+
+    def unpack(recv, side, ext, start):
+        for pair in range(RIM // 2):
+            both = recv[side, 2 * CRIT * pair : 2 * CRIT * (pair + 1), :].astype(jnp.float32)
+            ext[start + 2 * pair] = both[:CRIT]
+            ext[start + 2 * pair + 1] = both[CRIT:]
+
+    for side, start in ((0, 0), (1, nblk - RIM)):
         loads[side].wait()
-        start = 0 if side == 0 else cells - edge
-        for pair in range(RIM // 2):
-            at = start + 2 * pair * TILE
-            both = jnp.concatenate([xin[:, at : at + TILE], xin[:, at + TILE : at + 2 * TILE]], axis=0)
-            xsend[side, 2 * rows * pair : 2 * rows * (pair + 1), :] = both.astype(jnp.bfloat16)
-
-    pl.semaphore_wait(barrier, 2 + ncpl)
+        for b in range(start, start + RIM):
+            extend(b)
+        pack(xsend, side, xcrit, RIM + start)
+
+    pl.semaphore_wait(barrier, 1 + 2 * ncpl)
 
     def halo(send, recv, ssem, rsem, side):
         return pltpu.make_async_remote_copy(
@@ -157,40 +173,44 @@
         ).wait_recv()
 
     xhalos = [halo(xsend, xrecv, xs_sem, xr_sem, side) for side in range(2)]
+    yhalos = [
+        pltpu.make_async_remote_copy(
+            src_ref=xrest.at[pl.ds(RIM if side == 0 else nblk, RIM)],
+            dst_ref=xrest.at[pl.ds(RIM + nblk if side == 0 else 0, RIM)],
+            send_sem=ys_sem.at[side], recv_sem=yr_sem.at[side],
+            device_id={"dom": left if side == 0 else right}, device_id_type=MESH,
+        )
+        for side in range(2)
+    ]
     for copy in xhalos:
         copy.start()
     tabs = [cross(tab, lambda k: tab_recv.at[k], ts_sem, tr_sem, step) for step in range(ncpl)]
     for copy in tabs:
         copy.start()
 
+    for copy in yhalos:
+        copy.start()
+
     own_tab.wait()
     loads[2].wait()
 
-    def extend(group, carry):
+    def extend_eight(group, carry):
         for i in range(8):
-            b = group * 8 + i
-            xext[RIM + b] = xin[:, pl.ds(pl.multiple_of(b * TILE, TILE), TILE)]
-        return carry
-
-    lax.fori_loop(0, nblk // 8, extend, 0)
+            extend(group * 8 + i)
+        return carry
+
+    lax.fori_loop(RIM // 8, (nblk - RIM) // 8, extend_eight, 0)
     loads[3].wait()
     for side in range(2):
         xhalos[side].wait_recv()
-        start = RIM + nblk if side == 0 else 0
-        for pair in range(RIM // 2):
-            at = start + 2 * pair
-            both = xrecv[side, 2 * rows * pair : 2 * rows * (pair + 1), :].astype(jnp.float32)
-            xext[at] = both[:rows]
-            xext[at + 1] = both[rows:]
-
-    def state_product(j, carry):
-        piece = xext[ssrc[0, j]].astype(jnp.bfloat16)
-        product = jnp.dot(piece, wstate[j], preferred_element_type=jnp.float32)
-        pcrit[j] = product[:CRIT]
-        prest[j] = product[CRIT:]
-        return carry
-
-    lax.fori_loop(0, tpd, state_product, 0, unroll=True)
+        unpack(xrecv, side, xcrit, RIM + nblk if side == 0 else 0)
+
+    def crit_product(j, carry):
+        piece = xcrit[ssrc[0, j]].astype(jnp.bfloat16)
+        pcrit[j] = jnp.dot(piece, wstate[j], preferred_element_type=jnp.float32)
+        return carry
+
+    lax.fori_loop(0, tpd, crit_product, 0, unroll=True)
 
     def chain_crit(j, carry):
         pcrit[j] = pcrit[j] + pcrit[tab_own_s[1, j]]
@@ -204,6 +224,15 @@
     for copy in reversed(acopies):
         copy.start()
 
+    for copy in yhalos:
+        copy.wait_recv()
+
+    def rest_product(j, carry):
+        prest[j] = jnp.dot(xrest[ssrc[0, j]], wstate[j], preferred_element_type=jnp.float32)
+        return carry
+
+    lax.fori_loop(0, tpd, rest_product, 0, unroll=True)
+
     def chain_rest(j, carry):
         total = prest[j] + prest[tab_own_s[1, j]]
         prest[j] = total
@@ -212,9 +241,8 @@
 
     lax.fori_loop(0, tpd, chain_rest, 0, unroll=True)
     bdst = lambda k: brecv.at[k, pl.ds(0, tpd)]
-    bcopies = [cross(bsend, bdst, bs_sem, br_sem, step) for step in range(ncpl)]
-    for copy in reversed(bcopies):
-        copy.start()
+    bcopies = [cross(bsend, bdst, bs_sem, br_sem, 0)]
+    bcopies[0].start()
 
     tabcopies = []
     for k in range(ncpl):
@@ -270,14 +298,19 @@
 
     lax.fori_loop(1, nblk // 8 - 1, middle, 0)
 
+    arrived(bsend, bdst, bs_sem, br_sem, cpl)
+    for step in range(1, ncpl):
+        copy = pltpu.make_async_remote_copy(
+            src_ref=bdst(cpl), dst_ref=bdst(cpl), send_sem=bs_sem.at[step], recv_sem=br_sem.at[cpl],
+            device_id={"cpl": partners[step]}, device_id_type=MESH,
+        )
+        copy.start()
+        bcopies.append(copy)
+
     loads[4].wait()
     for side in range(2):
         fhalos[side].wait_recv()
-        base = RIM + nblk if side == 0 else 0
-        for pair in range(RIM // 2):
-            both = frecv[side, 2 * CRIT * pair : 2 * CRIT * (pair + 1), :].astype(jnp.float32)
-            fext[base + 2 * pair] = both[:CRIT]
-            fext[base + 2 * pair + 1] = both[CRIT:]
+        unpack(frecv, side, fext, RIM + nblk if side == 0 else 0)
 
     def flux_product(j, carry):
         piece = fext[fsrc[0, j]].astype(jnp.bfloat16)
@@ -298,8 +331,8 @@
     for copy in reversed(ccopies):
         copy.start()
 
-    for k in range(ncpl):
-        arrived(bsend, bdst, bs_sem, br_sem, k)
+    for partner in partners[1:]:
+        arrived(bsend, bdst, bs_sem, br_sem, partner)
 
     def place(group, carry):
         for i in range(8):
@@ -336,10 +369,26 @@
     store = pltpu.make_async_copy(fout, flux_hbm, out_sem.at[1])
     store.start()
 
-    for copy in xhalos + tabs + acopies + bcopies + fhalos + ccopies:
+    for copy in xhalos + yhalos + tabs + acopies + bcopies + fhalos + ccopies:
         copy.wait_send()
     deliver.wait()
     store.wait()
+
+
+def settle(rows, cells, deliv_in, flux_in, deliv_out, flux_out, sems):
+    half = cells // 2
+    parts = [(deliv_in, deliv_out, r, h) for r in range(0, rows, CRIT) for h in (0, half)]
+    parts += [(flux_in, flux_out, 0, h) for h in (0, half)]
+    copies = [
+        pltpu.make_async_copy(
+            src.at[pl.ds(r, CRIT), pl.ds(h, half)], dst.at[0, pl.ds(r, CRIT), pl.ds(h, half)], sems.at[i]
+        )
+        for i, (src, dst, r, h) in enumerate(parts)
+    ]
+    for copy in copies:
+        copy.start()
+    for copy in copies:
+        copy.wait()
 
 
 def body(ncpl, ndom, fields, wet_mask, wstate, ssrc, stgt, wflux, fsrc, ftgt):
@@ -361,7 +410,8 @@
         scratch_shapes=[pltpu.SMEM((1, tpd), i32)] * 4
         + [
             vmem((rows, cells), f32),
-            vmem((nblk + 2 * RIM, rows, TILE), f32),
+            vmem((nblk + 2 * RIM, CRIT, TILE), f32),
+            vmem((nblk + 2 * RIM, rest, TILE), bf16),
             vmem((nblk, TILE), i32),
             vmem((tpd, TILE, TILE), bf16),
             vmem((tpd, TILE, TILE), bf16),
@@ -373,8 +423,8 @@
             vmem((CRIT, cells), f32),
             vmem((8 * CRIT, TILE), f32),
             vmem((8 * CRIT, TILE), f32),
-            vmem((2, RIM * rows, TILE), bf16),
-            vmem((2, RIM * rows, TILE), bf16),
+            vmem((2, RIM * CRIT, TILE), bf16),
+            vmem((2, RIM * CRIT, TILE), bf16),
             vmem((2, RIM * CRIT, TILE), bf16),
             vmem((2, RIM * CRIT, TILE), bf16),
             vmem((8, 2 * nblk), i32),
@@ -390,7 +440,7 @@
             vmem((ncpl, tpd + 1, CRIT, TILE), f32),
             vmem((ncpl, tpd + 1, CRIT, TILE), f32),
             dma((10,)), dma((ncpl + 1,)), dma((2,)),
-            dma((2,)), dma((2,)), dma((2,)), dma((2,)),
+            dma((2,)), dma((2,)), dma((2,)), dma((2,)), dma((2,)), dma((2,)),
             dma((ncpl,)), dma((ncpl,)), dma((ncpl,)), dma((ncpl,)),
             dma((ncpl,)), dma((ncpl,)), dma((ncpl,)), dma((ncpl,)),
         ],
@@ -398,7 +448,16 @@
             collective_id=0, has_side_effects=True, vmem_limit_bytes=63 * 1024 * 1024
         ),
     )(ssrc, stgt, fsrc, ftgt, fields, wet_mask.reshape(nblk, TILE), wstate, wflux)
-    return delivered[None], fluxes[None]
+    return pl.pallas_call(
+        functools.partial(settle, rows, cells),
+        out_shape=(
+            jax.ShapeDtypeStruct((1, rows, cells), f32),
+            jax.ShapeDtypeStruct((1, CRIT, cells), f32),
+        ),
+        in_specs=[hbm_spec] * 2,
+        out_specs=(hbm_spec, hbm_spec),
+        scratch_shapes=[dma((2 * (rows // CRIT + 1),))],
+    )(delivered, fluxes)
 
 
 def solution(mesh):

time: 25.3 us -> 55.1 us (2.18)
  Pallas kernels: 21.7 us -> 54.3 us
  local copies, waits for them, and re-layouts: 2.81 us -> 0 us
    pallas_call x0 -> x1, Pallas kernels: none -> 32.9 us  [body(): pl.pallas_call(functools.partial(settle, rows, cells), out_shape=(jax.Sha...]
    unnamed x4 -> x0, local copies, waits for them, and re-layouts: 2.81 us -> none
where the time goes in v3:
time: 55.1 us; the launch traced here: 55 us
  Pallas kernels  54.3 us (99%)
  between operations  0.64 us (1%)
    pallas_call x1, Pallas kernels, body(): pl.pallas_call(functools.partial(settle, rows, cells), out_shape=(jax.Sha...  32.9 us
    pallas_call x1, Pallas kernels, body(): pl.pallas_call(functools.partial(kernel, (rows, nblk, tpd, ncpl, ndom)),...  21.4 us

profile of v3, /device:TPU:0, one launch (start us, length us, event | category | flops | bytes accessed | tf_op | source)
XLA Modules:
  0.0 55.0 jit_solution(12794526673859939410)
XLA Ops:
  0.6 21.4 %shard_map.95 = (f32[24,8192]{1,0:T(8,128)}, f32[8,8192]{1,0:T(8,128)}) custom-call(s32[1,24]{1,0:T(1,128)} %ssrc_hbm.1, s32[1,24]{1,0:T(1,128)} %stgt_hbm.1, s32[1,24]{1,0:T(1,128)} %fsrc_hbm.1, s32[1,24]{1,0:T(1,128)} %ftgt_hbm.1, f32[1,24,8192]{2,1,0:T(8,128)} %fields_hbm.1, s32[64,128]{1,0:T(8,128)} %bitcast.1, bf16[1,24,128,128]{3,2,1,0:T(8,128)(2,1)} %wstate_hbm.1, ...), custom_call_target="tpu_custom_call" | custom-call | tf_op jit(solution)/shard_map/pallas_call | solution.py:402
  22.0 32.9 %shard_map.96 = (f32[1,24,8192]{2,1,0:T(8,128)}, f32[1,8,8192]{2,1,0:T(8,128)}) custom-call(f32[24,8192]{1,0:T(8,128)} %get-tuple-element.4.deliv_in, f32[8,8192]{1,0:T(8,128)} %get-tuple-element.5.flux_in), custom_call_target="tpu_custom_call" | custom-call | tf_op jit(solution)/shard_map/pallas_call | solution.py:451

commit v4 on v3

--- a/solution.py
+++ b/solution.py
@@ -44,13 +44,13 @@
     sizes,
     ssrc_hbm, stgt_hbm, fsrc_hbm, ftgt_hbm,
     fields_hbm, wet_hbm, wstate_hbm, wflux_hbm,
-    deliv_hbm, flux_hbm,
+    dout, fout,
     ssrc, stgt, fsrc, ftgt,
-    xin, xcrit, xrest, wet, wstate, wflux, pcrit, prest, fbuf, fext, dout, fout, own_stage, got_stage,
+    xin, xcrit, xrest, wet, wstate, wflux, pcrit, prest, fbuf, fext, own_stage, got_stage,
     xsend, xrecv, fsend, frecv,
     tab, tab_recv, tab_own_s, tab_s,
     asend, arecv, bsend, brecv, csend, crecv, afull, cfull,
-    load_sem, tabcopy_sem, out_sem,
+    load_sem, tabcopy_sem,
     xs_sem, xr_sem, ys_sem, yr_sem, fs_sem, fr_sem,
     ts_sem, tr_sem, as_sem, ar_sem, bs_sem, br_sem, cs_sem, cr_sem,
 ):
@@ -344,8 +344,6 @@
         return carry
 
     lax.fori_loop(0, nblk // 8, place, 0)
-    deliver = pltpu.make_async_copy(dout, deliv_hbm, out_sem.at[0])
-    deliver.start()
 
     for k in range(ncpl):
         arrived(csend, lambda k: crecv.at[k], cs_sem, cr_sem, k)
@@ -366,13 +364,9 @@
         return carry
 
     lax.fori_loop(0, nblk // 8, merge, 0)
-    store = pltpu.make_async_copy(fout, flux_hbm, out_sem.at[1])
-    store.start()
 
     for copy in xhalos + yhalos + tabs + acopies + bcopies + fhalos + ccopies:
         copy.wait_send()
-    deliver.wait()
-    store.wait()
 
 
 def settle(rows, cells, deliv_in, flux_in, deliv_out, flux_out, sems):
@@ -399,14 +393,15 @@
     f32, bf16, i32 = jnp.float32, jnp.bfloat16, jnp.int32
     vmem, dma = pltpu.VMEM, pltpu.SemaphoreType.DMA
     hbm_spec = pl.BlockSpec(memory_space=pltpu.HBM)
+    vmem_spec = pl.BlockSpec(memory_space=pltpu.VMEM)
     delivered, fluxes = pl.pallas_call(
         functools.partial(kernel, (rows, nblk, tpd, ncpl, ndom)),
         out_shape=(
-            jax.ShapeDtypeStruct((rows, cells), f32),
-            jax.ShapeDtypeStruct((CRIT, cells), f32),
+            pltpu.VMEM((rows, cells), f32),
+            pltpu.VMEM((CRIT, cells), f32),
         ),
         in_specs=[hbm_spec] * 8,
-        out_specs=(hbm_spec, hbm_spec),
+        out_specs=(vmem_spec, vmem_spec),
         scratch_shapes=[pltpu.SMEM((1, tpd), i32)] * 4
         + [
             vmem((rows, cells), f32),
@@ -419,8 +414,6 @@
             vmem((tpd + 1, rest, TILE), f32),
             vmem((tpd + 1, CRIT, TILE), f32),
             vmem((nblk + 2 * RIM, CRIT, TILE), f32),
-            vmem((rows, cells), f32),
-            vmem((CRIT, cells), f32),
             vmem((8 * CRIT, TILE), f32),
             vmem((8 * CRIT, TILE), f32),
             vmem((2, RIM * CRIT, TILE), bf16),
@@ -439,13 +432,13 @@
             vmem((ncpl, tpd * CRIT, TILE), bf16),
             vmem((ncpl, tpd + 1, CRIT, TILE), f32),
             vmem((ncpl, tpd + 1, CRIT, TILE), f32),
-            dma((10,)), dma((ncpl + 1,)), dma((2,)),
+            dma((10,)), dma((ncpl + 1,)),
             dma((2,)), dma((2,)), dma((2,)), dma((2,)), dma((2,)), dma((2,)),
             dma((ncpl,)), dma((ncpl,)), dma((ncpl,)), dma((ncpl,)),
             dma((ncpl,)), dma((ncpl,)), dma((ncpl,)), dma((ncpl,)),
         ],
         compiler_params=pltpu.CompilerParams(
-            collective_id=0, has_side_effects=True, vmem_limit_bytes=63 * 1024 * 1024
+            collective_id=0, has_side_effects=True, vmem_limit_bytes=61 * 1024 * 1024
         ),
     )(ssrc, stgt, fsrc, ftgt, fields, wet_mask.reshape(nblk, TILE), wstate, wflux)
     return pl.pallas_call(
@@ -454,9 +447,10 @@
             jax.ShapeDtypeStruct((1, rows, cells), f32),
             jax.ShapeDtypeStruct((1, CRIT, cells), f32),
         ),
-        in_specs=[hbm_spec] * 2,
+        in_specs=[pl.BlockSpec(memory_space=pl.ANY)] * 2,
         out_specs=(hbm_spec, hbm_spec),
         scratch_shapes=[dma((2 * (rows // CRIT + 1),))],
+        compiler_params=pltpu.CompilerParams(vmem_limit_bytes=4 * 1024 * 1024),
     )(delivered, fluxes)
 
 

time: 55.1 us -> 22.5 us (0.41)
  Pallas kernels: 54.3 us -> 21.7 us
    pallas_call x1, Pallas kernels: 32.9 us -> 1.03 us  [body(): pl.pallas_call(functools.partial(settle, rows, cells), out_shape=(jax.Sha...]
    pallas_call x1, Pallas kernels: 21.4 us -> 20.7 us  [body(): pl.pallas_call(functools.partial(kernel, (rows, nblk, tpd, ncpl, ndom)),...]
where the time goes in v4:
time: 22.5 us; the launch traced here: 22.4 us
  Pallas kernels  21.7 us (96%)
  between operations  0.64 us (3%)
    pallas_call x1, Pallas kernels, body(): pl.pallas_call(functools.partial(kernel, (rows, nblk, tpd, ncpl, ndom)),...  20.7 us
    pallas_call x1, Pallas kernels, body(): pl.pallas_call(functools.partial(settle, rows, cells), out_shape=(jax.Sha...  1.03 us

profile of v4, /device:TPU:0, one launch (start us, length us, event | category | flops | bytes accessed | tf_op | source)
XLA Modules:
  0.0 22.4 jit_solution(9625724192960706313)
XLA Ops:
  0.6 20.7 %shard_map.95 = (f32[24,8192]{1,0:T(8,128)S(1)}, f32[8,8192]{1,0:T(8,128)S(1)}) custom-call(s32[1,24]{1,0:T(1,128)} %ssrc_hbm.1, s32[1,24]{1,0:T(1,128)} %stgt_hbm.1, s32[1,24]{1,0:T(1,128)} %fsrc_hbm.1, s32[1,24]{1,0:T(1,128)} %ftgt_hbm.1, f32[1,24,8192]{2,1,0:T(8,128)} %fields_hbm.1, s32[64,128]{1,0:T(8,128)} %bitcast.1, ...), custom_call_target="tpu_custom_call" | custom-call | tf_op jit(solution)/shard_map/pallas_call | solution.py:397
  21.3 1.0 %shard_map.96 = (f32[1,24,8192]{2,1,0:T(8,128)}, f32[1,8,8192]{2,1,0:T(8,128)}) custom-call(f32[24,8192]{1,0:T(8,128)S(1)} %get-tuple-element.4.deliv_in, f32[8,8192]{1,0:T(8,128)S(1)} %get-tuple-element.5.flux_in), custom_call_target="tpu_custom_call" | custom-call | tf_op jit(solution)/shard_map/pallas_call | solution.py:444
